TPU v7x, 32 devices: a whole 2x2x4 slice. The times are simulated.
32 devices in a mesh: groups: 2 (over x), blk: 16 (over z, y, core).
Axes of the slice: x: 2, y: 2, z: 4, core: 2. Of those that a mesh axis runs over, the one named last changes fastest.
Arguments:
- projections: bfloat16 [2, 512, 8192], P(None, ('groups', 'blk')), parts along dimension 1, may hold values from -12 to 12
- images: bfloat16 [64, 8192], P(('groups', 'blk')), parts along dimension 0, may hold values from -16 to 16, as said below
- ctf_group: int32 [64], P(('groups', 'blk')), parts along dimension 0, may hold values from 0 to 15
- shift_offsets: int32 [64, 9, 2], P(('groups', 'blk')), parts along dimension 0, may hold values from -8 to 8
- shell_limit: int32 [64], P(('groups', 'blk')), parts along dimension 0, may hold values from 16 to 63
- ctf_table: float32 [32, 4096], P('groups'), parts along dimension 0, may hold values from -1 to 1
- noise_weight: float32 [32, 4096], P('groups'), parts along dimension 0, may hold values from 0.25 to 4
Outputs:
- slices: float32 [2, 512, 8192], P(None, ('groups', 'blk')), parts along dimension 1
- best_posterior: float32 [64], P(('groups', 'blk')), parts along dimension 0
- log_total: float32 [64], P(('groups', 'blk')), parts along dimension 0
There are 2 independent parts, one for each index of `groups`. A program takes and returns all parts, laid end to end along the dimension named above; each array names one. Nothing has to cross between parts.
Inputs may be any that keep to these rules, and one draw needn't show every extreme that they name: `images`: image coefficients.
All inputs are finite; a program needn't handle non-finite values.
Results may differ from a plain program's by a relative error of at most 0.006.
Values may be sent and summed in bfloat16 or wider, within the bound.
No kernel may reach another device: no remote copies, remote signals or barrier semaphores. Data moves between devices by JAX's collectives and lax.ppermute only.
A program may use at most 128 MiB of HBM per device.

v0:
```python
import math
import jax
import jax.numpy as jnp
from jax import lax
from jax.sharding import PartitionSpec as P

KY = 64
IMG = 256


def combined_all(value, axis, join):
    pieces = jax.tree.map(lambda part: lax.all_gather(part, axis), value)
    head = jax.tree.map(lambda part: part[0], pieces)
    tail = jax.tree.map(lambda part: part[1:], pieces)
    so_far, _ = lax.scan(lambda so_far, section: (join(so_far, section), None), head, tail)
    return so_far


def frequencies(half_width):
    positions = jnp.arange(half_width, dtype=jnp.int32)
    return (positions // KY, positions % KY - KY // 2)


def shift_factors(offsets, half_width):
    row_count = offsets.shape[0]
    shift_count = offsets.shape[1]
    row_freq = jnp.arange(half_width // KY, dtype=jnp.int32)
    col_freq = jnp.arange(KY, dtype=jnp.int32) - KY // 2
    turns_x = row_freq[None, None, :] * offsets[:, :, 0:1] % IMG
    turns_y = col_freq[None, None, :] * offsets[:, :, 1:2] % IMG
    angle_x = turns_x.astype(jnp.float32) * (2.0 * math.pi / IMG)
    angle_y = turns_y.astype(jnp.float32) * (2.0 * math.pi / IMG)
    cosine_x = jnp.cos(angle_x)[:, :, :, None]
    sine_x = jnp.sin(angle_x)[:, :, :, None]
    cosine_y = jnp.cos(angle_y)[:, :, None, :]
    sine_y = jnp.sin(angle_y)[:, :, None, :]
    cosine = cosine_x * cosine_y - sine_x * sine_y
    sine_part = sine_x * cosine_y + cosine_x * sine_y
    return (
        cosine.reshape(row_count, shift_count, half_width),
        sine_part.reshape(row_count, shift_count, half_width),
    )


def particle_terms(image_rows, ctf_rows, weight_rows, offsets, limits, freq_x, freq_y):
    half_width = image_rows.shape[1] // 2
    image_real = image_rows[:, :half_width].astype(jnp.float32)
    image_imag = image_rows[:, half_width:].astype(jnp.float32)
    radius_sq = freq_x * freq_x + freq_y * freq_y
    inside = (radius_sq[None, :] < (limits * limits)[:, None]).astype(jnp.float32)
    masked_weight = inside * weight_rows
    ctf_weight = masked_weight * ctf_rows
    norm_term = jnp.sum(masked_weight * (image_real * image_real + image_imag * image_imag), axis=1)
    quad_weight = ctf_weight * ctf_rows
    cosine, sine_part = shift_factors(offsets, half_width)
    shift_real = image_real[:, None, :] * cosine + image_imag[:, None, :] * sine_part
    shift_imag = image_imag[:, None, :] * cosine - image_real[:, None, :] * sine_part
    weighted = jnp.concatenate(
        [ctf_weight[:, None, :] * shift_real, ctf_weight[:, None, :] * shift_imag], axis=2
    ).astype(jnp.bfloat16)
    return (weighted, norm_term, quad_weight)


def combine_lse(first, second):
    score_top = jnp.maximum(first[0], second[0])
    exp_total = first[1] * jnp.exp(first[0] - score_top) + second[1] * jnp.exp(
        second[0] - score_top
    )
    return (score_top, exp_total)


def block_shape(row_count):
    return 64 if row_count % 64 == 0 else row_count


def split_rows(members, block_rows):
    return tuple(
        (
            member.reshape((member.shape[0] // block_rows, block_rows) + member.shape[1:])
            for member in members
        )
    )


def local(projections, images, ctf_group, shift_offsets, shell_limit, ctf_table, noise_weight):
    batch_count, orient_dev, full_width = projections.shape
    half_width = full_width // 2
    candidates = batch_count * orient_dev
    flat_proj = projections.reshape(candidates, full_width)
    proj_real = flat_proj[:, :half_width].astype(jnp.float32)
    proj_imag = flat_proj[:, half_width:].astype(jnp.float32)
    proj_power = proj_real * proj_real + proj_imag * proj_imag
    freq_x, freq_y = frequencies(half_width)
    score_scale = 0.5 / math.sqrt(half_width)
    group_count = ctf_table.shape[0]
    particles_dev = images.shape[0]

    def block_terms(members):
        image_rows, groups, offsets, limits = members
        one_hot = (groups[:, None] == jnp.arange(group_count, dtype=jnp.int32)[None, :]).astype(
            jnp.float32
        )
        ctf_rows = jnp.dot(
            one_hot, ctf_table, precision=lax.Precision.HIGHEST, preferred_element_type=jnp.float32
        )
        weight_rows = jnp.dot(
            one_hot,
            noise_weight,
            precision=lax.Precision.HIGHEST,
            preferred_element_type=jnp.float32,
        )
        return particle_terms(image_rows, ctf_rows, weight_rows, offsets, limits, freq_x, freq_y)

    def score_block(members):
        weighted, norm_term, quad_weight = block_terms(members)
        cross_term = lax.dot_general(
            weighted, flat_proj, (((2,), (1,)), ((), ())), preferred_element_type=jnp.float32
        )
        quad_term = lax.dot_general(
            quad_weight,
            proj_power,
            (((1,), (1,)), ((), ())),
            precision=lax.Precision.HIGHEST,
            preferred_element_type=jnp.float32,
        )
        return -(norm_term[:, None, None] - 2.0 * cross_term + quad_term[:, None, :]) * score_scale

    members = (
        lax.all_gather(images, "blk", axis=0, tiled=True),
        lax.all_gather(ctf_group, "blk", axis=0, tiled=True),
        lax.all_gather(shift_offsets, "blk", axis=0, tiled=True),
        lax.all_gather(shell_limit, "blk", axis=0, tiled=True),
    )
    row_count = members[0].shape[0]
    block_rows = block_shape(row_count)
    blocks = lax.map(score_block, split_rows(members, block_rows))
    scores = blocks.reshape((row_count,) + blocks.shape[2:])
    local_top = jnp.max(scores, axis=(1, 2))
    local_total = jnp.sum(jnp.exp(scores - local_top[:, None, None]), axis=(1, 2))
    score_top, exp_total = combined_all((local_top, local_total), "blk", combine_lse)
    log_total = score_top + jnp.log(exp_total)
    pieces = (
        lax.all_gather(images, "blk", axis=0, tiled=True),
        lax.all_gather(ctf_group, "blk", axis=0, tiled=True),
        lax.all_gather(shift_offsets, "blk", axis=0, tiled=True),
        lax.all_gather(shell_limit, "blk", axis=0, tiled=True),
    )
    row_count = pieces[0].shape[0]
    block_rows = block_shape(row_count)

    def add_block(carry, packed):
        member_block, score_block_values, log_block = packed
        weighted = block_terms(member_block)[0]
        posterior = jnp.exp(score_block_values - log_block[:, None, None]).astype(jnp.bfloat16)
        contrib = lax.dot_general(
            posterior, weighted, (((0, 1), (0, 1)), ((), ())), preferred_element_type=jnp.float32
        )
        return (carry + contrib, None)

    zero_slices = jnp.zeros((candidates, full_width), jnp.float32)
    packed_scores = split_rows((scores, log_total), block_rows)
    summed, unused_out = lax.scan(
        add_block, zero_slices, (split_rows(pieces, block_rows), packed_scores[0], packed_scores[1])
    )
    slices = (summed * (candidates / particles_dev)).reshape(batch_count, orient_dev, full_width)
    own_start = lax.axis_index("blk") * particles_dev
    own_top = lax.dynamic_slice_in_dim(score_top, own_start, particles_dev, 0)
    own_log = lax.dynamic_slice_in_dim(log_total, own_start, particles_dev, 0)
    best_posterior = jnp.exp(own_top - own_log)
    return (slices, best_posterior, own_log)


def solution(mesh):
    in_specs = (
        P(None, ("groups", "blk"), None),
        P(("groups", "blk"), None),
        P(("groups", "blk")),
        P(("groups", "blk"), None, None),
        P(("groups", "blk")),
        P("groups", None),
        P("groups", None),
    )
    out_specs = (P(None, ("groups", "blk"), None), P(("groups", "blk")), P(("groups", "blk")))
    return jax.shard_map(local, mesh=mesh, in_specs=in_specs, out_specs=out_specs, check_vma=False)
```

profile of v0, /device:TPU:0, one launch (start us, length us, event | category | flops | bytes accessed | tf_op | source)
XLA Modules:
  0.0 127.0 jit_solution(18370479021721928491)
XLA Ops:
  0.6 23.6 %all_gather.31 = s32[32,9,2]{1,2,0:T(2,128)S(1)} all-gather(s32[2,9,2]{1,2,0:T(2,128)} %param.12), channel_id=1, replica_groups=mesh['groups'=2,'blk'=16] {'blk'}, dimensions={0}, use_global_device_ids=true | all-gather | bytes 2448 | tf_op jit(solution)/shard_map/all_gather | solution.py:145
  24.4 1.2 fusion.32
  25.6 7.2 %multiply_subtract_fusion = (f32[32,9,64,64]{3,2,0,1:T(8,128)}, f32[32,9,64,64]{3,2,0,1:T(8,128)}) fusion(f32[32,9,64]{2,0,1:T(8,128)S(1)} %get-tuple-element.134, f32[32,9,64]{2,0,1:T(8,128)S(1)} %get-tuple-element.140, f32[32,9,64]{2,0,1:T(8,128)S(1)} %get-tuple-element.133, f32[32,9,64]{2,0,1:T(8,128)S(1)} %get-tuple-element.141), kind=kLoop, calls=%fused_computation.8 | loop fusion | flops 7077888 | bytes 9732096 | tf_op jit(solution)/shard_map/while/body/eval_jaxpr/sub | solution.py:37
  32.8 8.3 %add.127 = f32[32,9,4096]{2,0,1:T(8,128)} reshape(f32[32,9,64,64]{3,2,0,1:T(8,128)} %get-tuple-element.126) | data formatting | bytes 9437184 | tf_op jit(solution)/shard_map/while/body/eval_jaxpr/add | solution.py:38
  41.1 8.4 %sub.78 = f32[32,9,4096]{2,0,1:T(8,128)} reshape(f32[32,9,64,64]{3,2,0,1:T(8,128)} %get-tuple-element.125) | data formatting | bytes 9437184 | tf_op jit(solution)/shard_map/while/body/eval_jaxpr/sub | solution.py:37
  49.5 18.8 %all-gather.2 = bf16[16,2,8192]{2,1,0:T(2,128)(2,1)S(1)} all-gather(bf16[1,2,8192]{2,1,0:T(2,128)(2,1)S(1)} %bitcast.43), channel_id=1, replica_groups=mesh['groups'=2,'blk'=16] {'blk'}, dimensions={0}, use_global_device_ids=true | all-gather | bytes 557056 | tf_op jit(solution)/shard_map/all_gather | solution.py:143
  68.3 0.2 reshape.156
  68.5 0.9 slice_convert_fusion.1
  69.4 0.6 dynamic-slice.6
  70.7 0.2 dynamic-update-slice
  70.9 0.2 dynamic-update-slice.1
  71.1 9.5 %all-reduce.4 = (s32[32]{0:T(128)S(1)}, s32[32]{0:T(128)S(1)}) all-reduce(s32[32]{0:T(128)S(1)} %dynamic-update-slice, s32[32]{0:T(128)S(1)} %dynamic-update-slice.1), channel_id=1, replica_groups=mesh['groups'=2,'blk'=16] {'blk'}, use_global_device_ids=true, to_apply=%add | all-reduce | flops 64 | bytes 512
  80.6 0.4 fusion.46
  81.1 0.6 multiply_reduce_fusion
  81.7 4.7 %multiply_convert_fusion.1 = (bf16[32,9,4096]{2,0,1:T(8,128)(2,1)S(1)}, bf16[32,9,4096]{2,0,1:T(8,128)(2,1)S(1)}) fusion(f32[32,9,4096]{2,0,1:T(8,128)} %add.127, f32[32,9,4096]{2,0,1:T(8,128)} %sub.78, f32[32,4096]{1,0:T(8,128)} %get-tuple-element.130, f32[32,4096]{1,0:T(8,128)S(1)} %get-tuple-element.129, f32[32,4096]{1,0:T(8,128)S(1)} %get-tuple-element.128), kind=kLoop, calls=%fused_computation.13 | loop fusion | flops 11796480 | bytes 15728640 | tf_op jit(solution)/shard_map/convert
  86.4 0.6 fusion.12
  87.0 3.5 %fusion.53 = (f32[32]{0:T(128)S(1)}, f32[32,9,32]{0,2,1:T(8,128)S(1)}) fusion(f32[32,32]{0,1:T(8,128)S(1)} %fusion.12, bf16[32,8192,1]{1,0,2:T(8,128)(2,1)S(1)} %bitcast.40, bf16[32,9,4096]{2,0,1:T(8,128)(2,1)S(1)} %get-tuple-element.124, bf16[32,9,4096]{2,0,1:T(8,128)(2,1)S(1)} %get-tuple-element.123, f32[32]{0:T(128)S(1)} %get-tuple-element.127), kind=kOutput, calls=%fused_computation.82 | convolution fusion | flops 160487392 | bytes 5284096 | tf_op jit(solution)/shard_map/while/body/eval_jaxpr/dot_general | solution.py:116
  91.2 0.2 dynamic-update-slice.2
  91.5 0.2 dynamic-update-slice.3
  91.7 30.1 %all-reduce.5 = (f32[512]{0:T(512)S(1)}, f32[512]{0:T(512)S(1)}) all-reduce(f32[512]{0:T(512)S(1)} %dynamic-update-slice.2, f32[512]{0:T(512)S(1)} %dynamic-update-slice.3), channel_id=2, replica_groups=mesh['groups'=2,'blk'=16] {'blk'}, use_global_device_ids=true, to_apply=%add.2 | all-reduce | flops 1024 | bytes 8192
  121.9 0.1 reshape.141
  122.1 0.6 while.2
  122.7 3.6 %fusion.5 = f32[32,8192]{1,0:T(8,128)} fusion(bf16[32,9,4096]{2,0,1:T(8,128)(2,1)} %copy-done.1, bf16[32,9,4096]{2,0,1:T(8,128)(2,1)S(1)} %get-tuple-element.123, f32[32,9,32]{0,2,1:T(8,128)S(1)} %get-tuple-element.139, f32[32]{0:T(128)S(1)} %log_add_fusion), kind=kOutput, calls=%fused_computation.10 | convolution fusion | flops 160712704 | bytes 5804160 | tf_op jit(solution)/shard_map/while/body/eval_jaxpr/dot_general | solution.py:155
  126.4 0.6 subtract_exponential_fusion
  (48 shorter events, 0.9 us)
Async XLA Ops:
  0.6 80.4 %copy-start = (f32[16,4096]{1,0:T(8,128)S(1)}, f32[16,4096]{1,0:T(8,128)}, u32[]{:S(2)}) copy-start(f32[16,4096]{1,0:T(8,128)} %param.15) | copy-start | bytes 786436
  41.1 8.4 %copy-start.4 = (bf16[2,8192]{1,0:T(2,128)(2,1)S(1)}, bf16[2,8192]{1,0:T(2,128)(2,1)}, u32[]{:S(2)}) copy-start(bf16[2,8192]{1,0:T(2,128)(2,1)} %param.10) | copy-start | bytes 98308
  41.1 28.3 %copy-start.7 = (u32[32]{0:T(128)S(1)}, u32[32]{0:T(128)}, u32[]{:S(2)}) copy-start(u32[32]{0:T(128)} %constant.138) | copy-start | bytes 388
  41.1 29.5 %copy-start.5 = (s32[2]{0:T(128)S(1)}, s32[2]{0:T(128)}, u32[]{:S(2)}) copy-start(s32[2]{0:T(128)} %param.13) | copy-start | bytes 28
  41.1 29.8 %copy-start.6 = (s32[2]{0:T(128)S(1)}, s32[2]{0:T(128)}, u32[]{:S(2)}) copy-start(s32[2]{0:T(128)} %param.11) | copy-start | bytes 28
  41.1 39.5 %copy-start.2 = (f32[16,4096]{1,0:T(8,128)S(1)}, f32[16,4096]{1,0:T(8,128)}, u32[]{:S(2)}) copy-start(f32[16,4096]{1,0:T(8,128)} %param.14) | copy-start | bytes 786436
  81.7 4.7 %copy-start.3 = (bf16[2,16,8192]{2,1,0:T(8,128)(2,1)S(1)}, bf16[2,16,8192]{2,1,0:T(8,128)(2,1)}, u32[]{:S(2)}) copy-start(bf16[2,16,8192]{2,1,0:T(8,128)(2,1)} %param.9) | copy-start | bytes 1572868
  86.3 4.2 %copy-start.1 = (bf16[32,9,4096]{2,0,1:T(8,128)(2,1)}, bf16[32,9,4096]{2,0,1:T(8,128)(2,1)S(1)}, u32[]{:S(2)}) copy-start(bf16[32,9,4096]{2,0,1:T(8,128)(2,1)S(1)} %get-tuple-element.124) | copy-start | bytes 7077892
where the time goes:
time: 127 us
  blocking collectives  81.9 us (64%)
  local copies, waits for them, and re-layouts  18.9 us (15%)
  other arithmetic  15 us (12%)
  matrix products  8.79 us (7%)
  between operations  2.1 us (2%)
    unnamed x2, blocking collectives  39.5 us
    all_gather x1, blocking collectives, local(): lax.all_gather(shift_offsets, 'blk', axis=0, tiled=True)  23.6 us
    all_gather x1, blocking collectives, local(): lax.all_gather(images, 'blk', axis=0, tiled=True)  18.8 us
    sub x1, local copies, waits for them, and re-layouts, shift_factors(): cosine = cosine_x * cosine_y - sine_x * sine_y  8.36 us
    add x1, local copies, waits for them, and re-layouts, shift_factors(): sine_part = sine_x * cosine_y + cosine_x * sine_y  8.32 us
    sub x1, other arithmetic, shift_factors(): cosine = cosine_x * cosine_y - sine_x * sine_y  7.17 us
    another operation x1, other arithmetic  4.66 us
    dot_general x1, matrix products, add_block(): lax.dot_general(posterior, weighted, (((0, 1), (0, 1)), ((), ())), prefer...  3.63 us

commit v1 on v0

--- a/solution.py
+++ b/solution.py
@@ -6,6 +6,28 @@
 
 KY = 64
 IMG = 256
+
+
+def joined_along(blocks, dim):
+    blocks = jnp.moveaxis(blocks, 0, dim)
+    dims = blocks.shape
+    return blocks.reshape(*dims[:dim], dims[dim] * dims[dim + 1], *dims[dim + 2 :])
+
+
+def gather_around(x, axis, dim):
+    count = lax.axis_size(axis)
+    pairs = [(i, (i + 1) % count) for i in range(count)]
+    back = [(b, a) for a, b in pairs]
+    lower, upper = ([], [])
+    for step in range(count - 1):
+        if step % 2 == 0:
+            lower.append(lax.ppermute(lower[-1] if lower else x, axis, pairs))
+        else:
+            upper.append(lax.ppermute(upper[-1] if upper else x, axis, back))
+    pieces = jnp.stack([*lower[::-1], x, *upper])
+    shift = lax.axis_index(axis) - len(lower)
+    pieces = pieces[(jnp.arange(count) - shift) % count]
+    return joined_along(pieces, dim)
 
 
 def combined_all(value, axis, join):
@@ -142,7 +164,7 @@
     pieces = (
         lax.all_gather(images, "blk", axis=0, tiled=True),
         lax.all_gather(ctf_group, "blk", axis=0, tiled=True),
-        lax.all_gather(shift_offsets, "blk", axis=0, tiled=True),
+        gather_around(shift_offsets, "blk", 0),
         lax.all_gather(shell_limit, "blk", axis=0, tiled=True),
     )
     row_count = pieces[0].shape[0]

time: 127 us -> 210 us (1.65)
  starting transfers between devices: 0 us -> 32.4 us
  local copies, waits for them, and re-layouts: 18.9 us -> 38.3 us
  other arithmetic: 15 us -> 28.4 us
  waiting for transfers between devices: 0 us -> 13.2 us
  blocking collectives: 81.9 us -> 84.6 us
    ppermute x0 -> x15, starting transfers between devices: none -> 32.4 us  [the longest x7 31.5 us: gather_around(): upper.append(lax.ppermute(upper[-1] if upper else x, axis, back))]
    ppermute x0 -> x15, waiting for transfers between devices: none -> 13.2 us  [the longest x8 12.9 us: gather_around(): lower.append(lax.ppermute(lower[-1] if lower else x, axis, pairs))]
    add x1 -> x2, local copies, waits for them, and re-layouts: 8.32 us -> 16.7 us  [shift_factors(): sine_part = sine_x * cosine_y + cosine_x * sine_y]
    sub x1 -> x2, local copies, waits for them, and re-layouts: 8.36 us -> 16.7 us  [shift_factors(): cosine = cosine_x * cosine_y - sine_x * sine_y]
    sub x1, other arithmetic: 7.17 us -> 13.9 us  [shift_factors(): cosine = cosine_x * cosine_y - sine_x * sine_y]
    another operation x1, other arithmetic: 4.66 us -> 9.76 us
    all_gather x1, blocking collectives: 18.8 us -> 23.8 us  [local(): lax.all_gather(images, 'blk', axis=0, tiled=True)]
    all_gather x1, blocking collectives: 23.6 us -> 19.6 us  [local(): lax.all_gather(shift_offsets, 'blk', axis=0, tiled=True)]
  transfers between devices with their start and end apart: 0 -> 15, of which waited for: 0 -> 7; matrix products, arithmetic and copies ran while one was open for 0% -> 4% of each run, Pallas kernels for 0% -> 0%
where the time goes in v1:
time: 210 us; the launch traced here: 209 us
  blocking collectives  84.6 us (40%)
  local copies, waits for them, and re-layouts  38.3 us (18%)
  starting transfers between devices  32.4 us (15%)
  other arithmetic  28.4 us (14%)
  waiting for transfers between devices  13.2 us (6%)
  matrix products  9.78 us (5%)
  between operations  2.19 us (1%)
    unnamed x2, blocking collectives  41.2 us
    ppermute x7, starting transfers between devices, gather_around(): upper.append(lax.ppermute(upper[-1] if upper else x, axis, back))  31.5 us
    all_gather x1, blocking collectives, local(): lax.all_gather(images, 'blk', axis=0, tiled=True)  23.8 us
    all_gather x1, blocking collectives, local(): lax.all_gather(shift_offsets, 'blk', axis=0, tiled=True)  19.6 us
    sub x2, local copies, waits for them, and re-layouts, shift_factors(): cosine = cosine_x * cosine_y - sine_x * sine_y  16.7 us
    add x2, local copies, waits for them, and re-layouts, shift_factors(): sine_part = sine_x * cosine_y + cosine_x * sine_y  16.7 us
    sub x1, other arithmetic, shift_factors(): cosine = cosine_x * cosine_y - sine_x * sine_y  13.9 us
    ppermute x8, waiting for transfers between devices, gather_around(): lower.append(lax.ppermute(lower[-1] if lower else x, axis, pairs))  12.9 us
  transfers between devices with their start and end apart: 15, of which 7 were waited for; matrix products, arithmetic and copies ran while one was open for 4% of the time, Pallas kernels for 0%

profile of v1, /device:TPU:0, one launch (start us, length us, event | category | flops | bytes accessed | tf_op | source)
XLA Modules:
  0.0 209.1 jit_solution(8113799220969559109)
XLA Ops:
  1.2 5.1 %collective-permute-start.8 = (s32[2,9,2]{1,2,0:T(2,128)}, s32[2,9,2]{1,2,0:T(2,128)S(1)}, u32[]{:S(2)}, u32[]{:S(2)}) collective-permute-start(s32[2,9,2]{1,2,0:T(2,128)} %param.12), channel_id=1, source_target_pairs={{1,0},{2,1},{3,2},{4,3},{5,4},{6,5},{7,6},{8,7},{9,8},{10,9},{11,1... | collective-permute-start | bytes 440 | tf_op jit(solution)/shard_map/ppermute | solution.py:26
  6.2 19.6 %all_gather.30 = s32[32,9,2]{1,2,0:T(2,128)S(1)} all-gather(s32[2,9,2]{1,2,0:T(2,128)} %param.12), channel_id=1, replica_groups=mesh['groups'=2,'blk'=16] {'blk'}, dimensions={0}, use_global_device_ids=true | all-gather | bytes 2448 | tf_op jit(solution)/shard_map/all_gather | solution.py:153
  30.4 7.5 %all-reduce.4 = (s32[32]{0:T(128)S(1)}, s32[32]{0:T(128)S(1)}) all-reduce(s32[32]{0:T(128)S(1)} %dynamic-update-slice, s32[32]{0:T(128)S(1)} %dynamic-update-slice.1), channel_id=1, replica_groups=mesh['groups'=2,'blk'=16] {'blk'}, use_global_device_ids=true, to_apply=%add | all-reduce | flops 64 | bytes 512
  37.9 23.8 %all-gather.2 = bf16[16,2,8192]{2,1,0:T(2,128)(2,1)S(1)} all-gather(bf16[1,2,8192]{2,1,0:T(2,128)(2,1)} %bitcast.91), channel_id=1, replica_groups=mesh['groups'=2,'blk'=16] {'blk'}, dimensions={0}, use_global_device_ids=true | all-gather | bytes 557056 | tf_op jit(solution)/shard_map/all_gather | solution.py:165
  63.6 1.4 fusion.75
  66.7 5.4 %collective-permute-done.1 = s32[2,9,2]{1,2,0:T(2,128)S(1)} collective-permute-done((s32[2,9,2]{1,2,0:T(2,128)S(1)}, s32[2,9,2]{1,2,0:T(2,128)S(1)}, u32[]{:S(2)}, u32[]{:S(2)}) %collective-permute-start.1) | collective-permute-done | bytes 176 | tf_op jit(solution)/shard_map/ppermute | solution.py:24
  72.0 4.4 %collective-permute-start.9 = (s32[2,9,2]{1,2,0:T(2,128)S(1)}, s32[2,9,2]{1,2,0:T(2,128)S(1)}, u32[]{:S(2)}, u32[]{:S(2)}) collective-permute-start(s32[2,9,2]{1,2,0:T(2,128)S(1)} %collective-permute-done.8), channel_id=1, source_target_pairs={{1,0},{2,1},{3,2},{4,3},{5,4},{6,5},{7,6},{8,7},{9,8},{10,9},{11,1... | collective-permute-start | bytes 440 | tf_op jit(solution)/shard_map/ppermute | solution.py:26
  76.5 1.3 collective-permute-done.2
  77.8 4.4 %collective-permute-start.10 = (s32[2,9,2]{1,2,0:T(2,128)S(1)}, s32[2,9,2]{1,2,0:T(2,128)S(1)}, u32[]{:S(2)}, u32[]{:S(2)}) collective-permute-start(s32[2,9,2]{1,2,0:T(2,128)S(1)} %collective-permute-done.9), channel_id=1, source_target_pairs={{1,0},{2,1},{3,2},{4,3},{5,4},{6,5},{7,6},{8,7},{9,8},{10,9},{11,1... | collective-permute-start | bytes 440 | tf_op jit(solution)/shard_map/ppermute | solution.py:26
  82.2 1.3 collective-permute-done.3
  83.5 4.4 %collective-permute-start.11 = (s32[2,9,2]{1,2,0:T(2,128)S(1)}, s32[2,9,2]{1,2,0:T(2,128)S(1)}, u32[]{:S(2)}, u32[]{:S(2)}) collective-permute-start(s32[2,9,2]{1,2,0:T(2,128)S(1)} %collective-permute-done.10), channel_id=1, source_target_pairs={{1,0},{2,1},{3,2},{4,3},{5,4},{6,5},{7,6},{8,7},{9,8},{10,9},{11,1... | collective-permute-start | bytes 440 | tf_op jit(solution)/shard_map/ppermute | solution.py:26
  87.9 1.3 collective-permute-done.4
  89.2 4.4 %collective-permute-start.12 = (s32[2,9,2]{1,2,0:T(2,128)S(1)}, s32[2,9,2]{1,2,0:T(2,128)S(1)}, u32[]{:S(2)}, u32[]{:S(2)}) collective-permute-start(s32[2,9,2]{1,2,0:T(2,128)S(1)} %collective-permute-done.11), channel_id=1, source_target_pairs={{1,0},{2,1},{3,2},{4,3},{5,4},{6,5},{7,6},{8,7},{9,8},{10,9},{11,1... | collective-permute-start | bytes 440 | tf_op jit(solution)/shard_map/ppermute | solution.py:26
  94.9 4.4 %collective-permute-start.13 = (s32[2,9,2]{1,2,0:T(2,128)S(1)}, s32[2,9,2]{1,2,0:T(2,128)S(1)}, u32[]{:S(2)}, u32[]{:S(2)}) collective-permute-start(s32[2,9,2]{1,2,0:T(2,128)S(1)} %collective-permute-done.12), channel_id=1, source_target_pairs={{1,0},{2,1},{3,2},{4,3},{5,4},{6,5},{7,6},{8,7},{9,8},{10,9},{11,1... | collective-permute-start | bytes 440 | tf_op jit(solution)/shard_map/ppermute | solution.py:26
  100.6 4.4 %collective-permute-start.14 = (s32[2,9,2]{1,2,0:T(2,128)S(1)}, s32[2,9,2]{1,2,0:T(2,128)S(1)}, u32[]{:S(2)}, u32[]{:S(2)}) collective-permute-start(s32[2,9,2]{1,2,0:T(2,128)S(1)} %collective-permute-done.13), channel_id=1, source_target_pairs={{1,0},{2,1},{3,2},{4,3},{5,4},{6,5},{7,6},{8,7},{9,8},{10,9},{11,1... | collective-permute-start | bytes 440 | tf_op jit(solution)/shard_map/ppermute | solution.py:26
  109.1 13.9 %multiply_subtract_fusion = (f32[32,9,64,64]{3,2,0,1:T(8,128)}, f32[32,9,64,64]{3,2,0,1:T(8,128)}, f32[32,9,64,64]{3,2,0,1:T(8,128)}, f32[32,9,64,64]{3,2,0,1:T(8,128)}) fusion(f32[32,9,64]{2,0,1:T(8,128)S(1)} %get-tuple-element.149, f32[32,9,64]{2,0,1:T(8,128)S(1)} %get-tuple-element.148, f32[32,9,64]{2,0,1:T(8,128)S(1)} %get-tuple-element.150, ...), kind=kLoop, calls=%fused_computation.9 | loop fusion | flops 14155776 | bytes 19464192 | tf_op jit(solution)/shard_map/while/body/eval_jaxpr/sub | solution.py:59
  123.1 8.3 %add.177 = f32[32,9,4096]{2,0,1:T(8,128)} reshape(f32[32,9,64,64]{3,2,0,1:T(8,128)} %get-tuple-element.154) | data formatting | bytes 9437184 | tf_op jit(solution)/shard_map/while/body/eval_jaxpr/add | solution.py:60
  131.4 8.3 %add.188 = f32[32,9,4096]{2,0,1:T(8,128)} reshape(f32[32,9,64,64]{3,2,0,1:T(8,128)} %get-tuple-element.132) | data formatting | bytes 9437184 | tf_op jit(solution)/shard_map/while/body/eval_jaxpr/add | solution.py:60
  139.7 8.3 %sub.104 = f32[32,9,4096]{2,0,1:T(8,128)} reshape(f32[32,9,64,64]{3,2,0,1:T(8,128)} %get-tuple-element.155) | data formatting | bytes 9437184 | tf_op jit(solution)/shard_map/while/body/eval_jaxpr/sub | solution.py:59
  148.1 8.3 %sub.115 = f32[32,9,4096]{2,0,1:T(8,128)} reshape(f32[32,9,64,64]{3,2,0,1:T(8,128)} %get-tuple-element.131) | data formatting | bytes 9437184 | tf_op jit(solution)/shard_map/while/body/eval_jaxpr/sub | solution.py:59
  156.4 9.8 %multiply_convert_fusion.3 = (bf16[32,9,4096]{2,0,1:T(8,128)(2,1)S(1)}, bf16[32,9,4096]{2,0,1:T(8,128)(2,1)S(1)}, bf16[32,9,4096]{2,0,1:T(8,128)(2,1)S(1)}, bf16[32,9,4096]{2,0,1:T(8,128)(2,1)}) fusion(f32[32,9,4096]{2,0,1:T(8,128)} %add.177, f32[32,9,4096]{2,0,1:T(8,128)} %sub.104, f32[32,4096]{1,0:T(8,128)} %get-tuple-element.136, ...), kind=kLoop, calls=%fused_computation.24 | loop fusion | flops 23592960 | bytes 29884416 | tf_op jit(solution)/shard_map/convert.2
  166.2 3.5 %fusion.85 = (f32[32]{0:T(128)S(1)}, f32[32,9,32]{0,2,1:T(8,128)S(1)}) fusion(f32[32,32]{0,1:T(8,128)S(1)} %fusion.28, bf16[32,8192,1]{1,0,2:T(8,128)(2,1)S(1)} %bitcast.86, bf16[32,9,4096]{2,0,1:T(8,128)(2,1)S(1)} %get-tuple-element.124, bf16[32,9,4096]{2,0,1:T(8,128)(2,1)S(1)} %get-tuple-element.123, f32[32]{0:T(128)S(1)} %get-tuple-element.133), kind=kOutput, calls=%fused_computation.137 | convolution fusion | flops 160487392 | bytes 5284096 | tf_op jit(solution)/shard_map/while/body/eval_jaxpr/dot_general | solution.py:138
  170.2 33.7 %all-reduce.5 = (f32[512]{0:T(512)S(1)}, f32[512]{0:T(512)S(1)}) all-reduce(f32[512]{0:T(512)S(1)} %dynamic-update-slice.2, f32[512]{0:T(512)S(1)} %dynamic-update-slice.3), channel_id=2, replica_groups=mesh['groups'=2,'blk'=16] {'blk'}, use_global_device_ids=true, to_apply=%add.2 | all-reduce | flops 1024 | bytes 8192
  205.5 3.6 %fusion.5 = f32[32,8192]{1,0:T(8,128)} fusion(bf16[32,9,4096]{2,0,1:T(8,128)(2,1)S(1)} %get-tuple-element.127, bf16[32,9,4096]{2,0,1:T(8,128)(2,1)} %get-tuple-element.128, f32[32,9,32]{0,2,1:T(8,128)S(1)} %get-tuple-element.153, f32[32]{0:T(128)S(1)} %log_add_fusion), kind=kOutput, calls=%fused_computation.13 | convolution fusion | flops 160712704 | bytes 5804160 | tf_op jit(solution)/shard_map/while/body/eval_jaxpr/dot_general | solution.py:177
  (98 shorter events, 16.6 us)
Async XLA Ops:
  0.6 64.3 %copy-start = (f32[16,4096]{1,0:T(8,128)S(1)}, f32[16,4096]{1,0:T(8,128)}, u32[]{:S(2)}) copy-start(f32[16,4096]{1,0:T(8,128)} %param.15) | copy-start | bytes 786436
  0.6 105.7 %copy-start.4 = (s32[2,9,2]{1,2,0:T(2,128)S(1)}, s32[2,9,2]{1,2,0:T(2,128)}, u32[]{:S(2)}) copy-start(s32[2,9,2]{1,2,0:T(2,128)} %param.12) | copy-start | bytes 436
  0.7 64.9 %copy-start.2 = (bf16[2,16,8192]{2,1,0:T(8,128)(2,1)S(1)}, bf16[2,16,8192]{2,1,0:T(8,128)(2,1)}, u32[]{:S(2)}) copy-start(bf16[2,16,8192]{2,1,0:T(8,128)(2,1)} %param.9) | copy-start | bytes 1572868
  0.7 65.6 %collective-permute-start = (s32[2,9,2]{1,2,0:T(2,128)}, s32[2,9,2]{1,2,0:T(2,128)S(1)}, u32[]{:S(2)}, u32[]{:S(2)}) collective-permute-start(s32[2,9,2]{1,2,0:T(2,128)} %param.12), channel_id=1, source_target_pairs={{0,1},{1,2},{2,3},{3,4},{4,5},{5,6},{6,7},{7,8},{8,9},{9,10},{10,1... | collective-permute-start | bytes 440 | tf_op jit(solution)/shard_map/ppermute | solution.py:24
  1.2 70.8 %collective-permute-start.8 = (s32[2,9,2]{1,2,0:T(2,128)}, s32[2,9,2]{1,2,0:T(2,128)S(1)}, u32[]{:S(2)}, u32[]{:S(2)}) collective-permute-start(s32[2,9,2]{1,2,0:T(2,128)} %param.12), channel_id=1, source_target_pairs={{1,0},{2,1},{3,2},{4,3},{5,4},{6,5},{7,6},{8,7},{9,8},{10,9},{11,1... | collective-permute-start | bytes 440 | tf_op jit(solution)/shard_map/ppermute | solution.py:26
  66.3 5.8 %collective-permute-start.1 = (s32[2,9,2]{1,2,0:T(2,128)S(1)}, s32[2,9,2]{1,2,0:T(2,128)S(1)}, u32[]{:S(2)}, u32[]{:S(2)}) collective-permute-start(s32[2,9,2]{1,2,0:T(2,128)S(1)} %collective-permute-done), channel_id=1, source_target_pairs={{0,1},{1,2},{2,3},{3,4},{4,5},{5,6},{6,7},{7,8},{8,9},{9,10},{10,1... | collective-permute-start | bytes 440 | tf_op jit(solution)/shard_map/ppermute | solution.py:24
  72.0 5.7 %collective-permute-start.2 = (s32[2,9,2]{1,2,0:T(2,128)S(1)}, s32[2,9,2]{1,2,0:T(2,128)S(1)}, u32[]{:S(2)}, u32[]{:S(2)}) collective-permute-start(s32[2,9,2]{1,2,0:T(2,128)S(1)} %collective-permute-done.1), channel_id=1, source_target_pairs={{0,1},{1,2},{2,3},{3,4},{4,5},{5,6},{6,7},{7,8},{8,9},{9,10},{10,1... | collective-permute-start | bytes 440 | tf_op jit(solution)/shard_map/ppermute | solution.py:24
  72.0 5.8 %collective-permute-start.9 = (s32[2,9,2]{1,2,0:T(2,128)S(1)}, s32[2,9,2]{1,2,0:T(2,128)S(1)}, u32[]{:S(2)}, u32[]{:S(2)}) collective-permute-start(s32[2,9,2]{1,2,0:T(2,128)S(1)} %collective-permute-done.8), channel_id=1, source_target_pairs={{1,0},{2,1},{3,2},{4,3},{5,4},{6,5},{7,6},{8,7},{9,8},{10,9},{11,1... | collective-permute-start | bytes 440 | tf_op jit(solution)/shard_map/ppermute | solution.py:26
  77.7 5.7 %collective-permute-start.3 = (s32[2,9,2]{1,2,0:T(2,128)S(1)}, s32[2,9,2]{1,2,0:T(2,128)S(1)}, u32[]{:S(2)}, u32[]{:S(2)}) collective-permute-start(s32[2,9,2]{1,2,0:T(2,128)S(1)} %collective-permute-done.2), channel_id=1, source_target_pairs={{0,1},{1,2},{2,3},{3,4},{4,5},{5,6},{6,7},{7,8},{8,9},{9,10},{10,1... | collective-permute-start | bytes 440 | tf_op jit(solution)/shard_map/ppermute | solution.py:24
  77.8 5.7 %collective-permute-start.10 = (s32[2,9,2]{1,2,0:T(2,128)S(1)}, s32[2,9,2]{1,2,0:T(2,128)S(1)}, u32[]{:S(2)}, u32[]{:S(2)}) collective-permute-start(s32[2,9,2]{1,2,0:T(2,128)S(1)} %collective-permute-done.9), channel_id=1, source_target_pairs={{1,0},{2,1},{3,2},{4,3},{5,4},{6,5},{7,6},{8,7},{9,8},{10,9},{11,1... | collective-permute-start | bytes 440 | tf_op jit(solution)/shard_map/ppermute | solution.py:26
  83.4 5.7 %collective-permute-start.4 = (s32[2,9,2]{1,2,0:T(2,128)S(1)}, s32[2,9,2]{1,2,0:T(2,128)S(1)}, u32[]{:S(2)}, u32[]{:S(2)}) collective-permute-start(s32[2,9,2]{1,2,0:T(2,128)S(1)} %collective-permute-done.3), channel_id=1, source_target_pairs={{0,1},{1,2},{2,3},{3,4},{4,5},{5,6},{6,7},{7,8},{8,9},{9,10},{10,1... | collective-permute-start | bytes 440 | tf_op jit(solution)/shard_map/ppermute | solution.py:24
  83.5 5.7 %collective-permute-start.11 = (s32[2,9,2]{1,2,0:T(2,128)S(1)}, s32[2,9,2]{1,2,0:T(2,128)S(1)}, u32[]{:S(2)}, u32[]{:S(2)}) collective-permute-start(s32[2,9,2]{1,2,0:T(2,128)S(1)} %collective-permute-done.10), channel_id=1, source_target_pairs={{1,0},{2,1},{3,2},{4,3},{5,4},{6,5},{7,6},{8,7},{9,8},{10,9},{11,1... | collective-permute-start | bytes 440 | tf_op jit(solution)/shard_map/ppermute | solution.py:26
  89.1 5.7 %collective-permute-start.5 = (s32[2,9,2]{1,2,0:T(2,128)S(1)}, s32[2,9,2]{1,2,0:T(2,128)S(1)}, u32[]{:S(2)}, u32[]{:S(2)}) collective-permute-start(s32[2,9,2]{1,2,0:T(2,128)S(1)} %collective-permute-done.4), channel_id=1, source_target_pairs={{0,1},{1,2},{2,3},{3,4},{4,5},{5,6},{6,7},{7,8},{8,9},{9,10},{10,1... | collective-permute-start | bytes 440 | tf_op jit(solution)/shard_map/ppermute | solution.py:24
  89.2 5.7 %collective-permute-start.12 = (s32[2,9,2]{1,2,0:T(2,128)S(1)}, s32[2,9,2]{1,2,0:T(2,128)S(1)}, u32[]{:S(2)}, u32[]{:S(2)}) collective-permute-start(s32[2,9,2]{1,2,0:T(2,128)S(1)} %collective-permute-done.11), channel_id=1, source_target_pairs={{1,0},{2,1},{3,2},{4,3},{5,4},{6,5},{7,6},{8,7},{9,8},{10,9},{11,1... | collective-permute-start | bytes 440 | tf_op jit(solution)/shard_map/ppermute | solution.py:26
  94.8 5.7 %collective-permute-start.6 = (s32[2,9,2]{1,2,0:T(2,128)S(1)}, s32[2,9,2]{1,2,0:T(2,128)S(1)}, u32[]{:S(2)}, u32[]{:S(2)}) collective-permute-start(s32[2,9,2]{1,2,0:T(2,128)S(1)} %collective-permute-done.5), channel_id=1, source_target_pairs={{0,1},{1,2},{2,3},{3,4},{4,5},{5,6},{6,7},{7,8},{8,9},{9,10},{10,1... | collective-permute-start | bytes 440 | tf_op jit(solution)/shard_map/ppermute | solution.py:24
  94.9 5.7 %collective-permute-start.13 = (s32[2,9,2]{1,2,0:T(2,128)S(1)}, s32[2,9,2]{1,2,0:T(2,128)S(1)}, u32[]{:S(2)}, u32[]{:S(2)}) collective-permute-start(s32[2,9,2]{1,2,0:T(2,128)S(1)} %collective-permute-done.12), channel_id=1, source_target_pairs={{1,0},{2,1},{3,2},{4,3},{5,4},{6,5},{7,6},{8,7},{9,8},{10,9},{11,1... | collective-permute-start | bytes 440 | tf_op jit(solution)/shard_map/ppermute | solution.py:26
  100.6 5.7 %collective-permute-start.7 = (s32[2,9,2]{1,2,0:T(2,128)S(1)}, s32[2,9,2]{1,2,0:T(2,128)S(1)}, u32[]{:S(2)}, u32[]{:S(2)}) collective-permute-start(s32[2,9,2]{1,2,0:T(2,128)S(1)} %collective-permute-done.6), channel_id=1, source_target_pairs={{0,1},{1,2},{2,3},{3,4},{4,5},{5,6},{6,7},{7,8},{8,9},{9,10},{10,1... | collective-permute-start | bytes 440 | tf_op jit(solution)/shard_map/ppermute | solution.py:24
  100.6 5.8 %collective-permute-start.14 = (s32[2,9,2]{1,2,0:T(2,128)S(1)}, s32[2,9,2]{1,2,0:T(2,128)S(1)}, u32[]{:S(2)}, u32[]{:S(2)}) collective-permute-start(s32[2,9,2]{1,2,0:T(2,128)S(1)} %collective-permute-done.13), channel_id=1, source_target_pairs={{1,0},{2,1},{3,2},{4,3},{5,4},{6,5},{7,6},{8,7},{9,8},{10,9},{11,1... | collective-permute-start | bytes 440 | tf_op jit(solution)/shard_map/ppermute | solution.py:26
  156.4 9.8 %copy-start.3 = (bf16[2,16,8192]{2,1,0:T(8,128)(2,1)S(1)}, bf16[2,16,8192]{2,1,0:T(8,128)(2,1)}, u32[]{:S(2)}) copy-start(bf16[2,16,8192]{2,1,0:T(8,128)(2,1)} %param.9) | copy-start | bytes 1572868
  166.2 42.9 %copy-start.1 = (f32[16,4096]{1,0:T(8,128)S(1)}, f32[16,4096]{1,0:T(8,128)}, u32[]{:S(2)}) copy-start(f32[16,4096]{1,0:T(8,128)} %param.15) | copy-start | bytes 786436
